TPU v7x, 32 devices: a whole 2x2x4 slice. The times are simulated.
32 devices in a mesh: ctx: 8 (over y, x, core), fsdp: 4 (over z).
Axes of the slice: x: 2, y: 2, z: 4, core: 2. Of those that a mesh axis runs over, the one named last changes fastest.
Arguments:
- tokens: bfloat16 [4, 4096, 512], P('fsdp', 'ctx'), may hold values from -6 to 6
- cotangent: bfloat16 [4, 4096, 512], P('fsdp', 'ctx'), may hold values from -6 to 6
- block_table: int32 [16], replicated, may hold values from 0 to 15, as said below
- seg_ids: int32 [4, 4096], P('fsdp'), may hold values from 0 to 2, as said below
- group_ids: int32 [4, 4096], P('fsdp', 'ctx'), may hold values from 0 to 127, as said below
- w_qkv: bfloat16 [512, 1536], P('fsdp'), may hold values from -0.375 to 0.375
- w_out: bfloat16 [512, 512], P('fsdp'), may hold values from -1.5 to 1.5
- w_router: bfloat16 [512, 8], P('fsdp'), may hold values from -0.1875 to 0.1875
- ln_gain: bfloat16 [512], P('fsdp'), may hold values from 0.5 to 1.5
- ln_bias: bfloat16 [512], P('fsdp'), may hold values from -1 to 1
- w_up: bfloat16 [8, 512, 2048], P('fsdp'), may hold values from -2 to 2
- w_down: bfloat16 [8, 2048, 512], P('fsdp'), may hold values from -1.5 to 1.5
Outputs:
- layer_out: float32 [4, 4096, 512], P('fsdp', 'ctx')
- grad_tokens: float32 [4, 4096, 512], P('fsdp', 'ctx')
- grad_qkv: float32 [512, 1536], P('fsdp')
- grad_out: float32 [512, 512], P('fsdp')
- grad_router: float32 [512, 8], P('fsdp')
- grad_gain: float32 [512], P('fsdp')
- grad_bias: float32 [512], P('fsdp')
- grad_up: float32 [8, 512, 2048], P('fsdp')
- grad_down: float32 [8, 2048, 512], P('fsdp')
Inputs may be any that keep to these rules, and one draw needn't show every extreme that they name: `block_table`: a permutation; each index c of ctx holds stored blocks 2c and 2c + 1, which are sequence blocks j and 15 - j for some j. `seg_ids`: in sequence order each batch is the prompt (segment 0) followed by continuations 1 to 2, each a nonempty run of positions. `group_ids`: every group has exactly 32 tokens; the tokens of ctx index c have groups c * 16 to (c + 1) * 16 - 1.
All inputs are finite; a program needn't handle non-finite values.
Results may differ from a plain program's by a relative error of at most 0.019.
Values may be sent and summed in bfloat16 or wider, within the bound.
A program may use at most 256 MiB of HBM per device.

v0:
```python
import functools

import jax
import jax.numpy as jnp
from jax import lax
from jax.experimental import pallas as pl
from jax.experimental.pallas import tpu as pltpu
from jax.sharding import PartitionSpec as P

HEADS = 8
HEAD = 64
GROUP_SIZE = 32
KEY_BLOCK = 2048


highest = lax.Precision.HIGHEST
neg_large = -1e30
epsilon = 1e-05
gelu_coef = 0.7978845608028654
gelu_cubic = 0.044715


def contract_rows(left, right):
    return lax.dot_general(
        left, right, (((0,), (0,)), ((), ())), preferred_element_type=jnp.float32
    )


def contract_cols(left, right):
    return lax.dot_general(
        left, right, (((1,), (1,)), ((), ())), preferred_element_type=jnp.float32
    )


def gelu_slope(value):
    inner = gelu_coef * (value + gelu_cubic * value * value * value)
    tangent = jnp.tanh(inner)
    return 0.5 * (1.0 + tangent) + 0.5 * value * (1.0 - tangent * tangent) * gelu_coef * (
        1.0 + 3.0 * gelu_cubic * value * value
    )


def expert_forward(mixed_low, up_weight, down_weight):
    pre = jnp.einsum("ged,edh->geh", mixed_low, up_weight, preferred_element_type=jnp.float32)
    active = jax.nn.gelu(pre, approximate=True).astype(jnp.bfloat16)
    result = jnp.einsum("geh,ehd->ged", active, down_weight, preferred_element_type=jnp.float32)
    return (pre, active, result.astype(jnp.bfloat16))


def expert_backward(mixed_low, pre, active, grad_result, up_weight, down_weight):
    grad_act = jnp.einsum(
        "ged,ehd->geh", grad_result, down_weight, preferred_element_type=jnp.float32
    )
    grad_pre = (grad_act * gelu_slope(pre)).astype(jnp.bfloat16)
    grad_down_part = jnp.einsum(
        "geh,ged->ehd", active, grad_result, preferred_element_type=jnp.float32
    )
    grad_up_part = jnp.einsum(
        "ged,geh->edh", mixed_low, grad_pre, preferred_element_type=jnp.float32
    )
    grad_mixed = jnp.einsum("geh,edh->ged", grad_pre, up_weight, preferred_element_type=jnp.float32)
    return (grad_up_part, grad_down_part, grad_mixed.astype(jnp.bfloat16))


def on_device(
    tokens,
    cotangent,
    block_table,
    seg_ids,
    group_ids,
    w_qkv,
    w_out,
    w_router,
    ln_gain,
    ln_bias,
    w_up,
    w_down,
):
    tok_rows = tokens[0]
    tok_count = tok_rows.shape[0]
    width = tok_rows.shape[1]
    expert_count = w_router.shape[1]
    ctx_index = lax.axis_index("ctx")
    full_rows = seg_ids.shape[1]
    block_len = full_rows // block_table.shape[0]
    row_ids = jnp.arange(full_rows, dtype=jnp.int32)
    key_pos = jnp.take(block_table, row_ids // block_len) * block_len + row_ids % block_len
    key_seg = seg_ids[0]
    pos_rows = lax.dynamic_slice_in_dim(key_pos, ctx_index * tok_count, tok_count)
    seg_rows = lax.dynamic_slice_in_dim(key_seg, ctx_index * tok_count, tok_count)
    scale = HEAD ** (-0.5)
    qkv_full, out_full, router_full, gain_full, bias_full = (
        lax.all_gather(w_qkv, "fsdp", axis=0, tiled=True),
        lax.all_gather(w_out, "fsdp", axis=0, tiled=True),
        lax.all_gather(w_router, "fsdp", axis=0, tiled=True),
        lax.all_gather(ln_gain, "fsdp", axis=0, tiled=True),
        lax.all_gather(ln_bias, "fsdp", axis=0, tiled=True),
    )
    qkv = jnp.dot(tok_rows, qkv_full, preferred_element_type=jnp.float32).astype(jnp.bfloat16)
    query_heads = qkv[:, :width].reshape(tok_count, HEADS, HEAD)
    key_all, val_all = (
        lax.all_gather(qkv[:, width : 2 * width], "ctx", axis=0, tiled=True),
        lax.all_gather(qkv[:, 2 * width :], "ctx", axis=0, tiled=True),
    )
    key_heads = key_all.reshape(full_rows, HEADS, HEAD)
    val_heads = val_all.reshape(full_rows, HEADS, HEAD)
    block_count = full_rows // KEY_BLOCK
    block_ids = jnp.arange(block_count, dtype=jnp.int32)

    def block_scores(index):
        start = index * KEY_BLOCK
        key_block = lax.dynamic_slice_in_dim(key_heads, start, KEY_BLOCK, 0)
        val_block = lax.dynamic_slice_in_dim(val_heads, start, KEY_BLOCK, 0)
        pos_block = lax.dynamic_slice_in_dim(key_pos, start, KEY_BLOCK, 0)
        seg_block = lax.dynamic_slice_in_dim(key_seg, start, KEY_BLOCK, 0)
        scores = (
            jnp.einsum("qhd,khd->hqk", query_heads, key_block, preferred_element_type=jnp.float32)
            * scale
        )
        allowed = (pos_block[None, :] <= pos_rows[:, None]) & (
            (seg_block[None, :] == 0) | (seg_block[None, :] == seg_rows[:, None])
        )
        return (scores, allowed[None], key_block, val_block)

    def lse_step(carry, index):
        top, total = carry
        scores, allowed, key_block, val_block = block_scores(index)
        masked = jnp.where(allowed, scores, neg_large)
        new_top = jnp.maximum(top, jnp.max(masked, axis=-1))
        weights = jnp.where(allowed, jnp.exp(masked - new_top[..., None]), 0.0)
        return ((new_top, total * jnp.exp(top - new_top) + jnp.sum(weights, axis=-1)), None)

    start_top = jnp.full((HEADS, tok_count), neg_large, jnp.float32)
    (top, total), unused = lax.scan(
        lse_step, (start_top, jnp.zeros((HEADS, tok_count), jnp.float32)), block_ids
    )
    log_total = top + jnp.log(total)

    def block_probs(index):
        scores, allowed, key_block, val_block = block_scores(index)
        probs = jnp.where(allowed, jnp.exp(scores - log_total[..., None]), 0.0)
        return (probs, key_block, val_block)

    def value_step(accum, index):
        probs, key_block, val_block = block_probs(index)
        return (
            accum
            + jnp.einsum(
                "hqk,khd->qhd",
                probs.astype(jnp.bfloat16),
                val_block,
                preferred_element_type=jnp.float32,
            ),
            None,
        )

    accum, unused = lax.scan(
        value_step, jnp.zeros((tok_count, HEADS, HEAD), jnp.float32), block_ids
    )
    attended = accum.reshape(tok_count, width).astype(jnp.bfloat16)
    hidden = tok_rows.astype(jnp.float32) + jnp.dot(
        attended, out_full, preferred_element_type=jnp.float32
    )
    center = hidden - jnp.mean(hidden, axis=-1, keepdims=True)
    inv_dev = lax.rsqrt(jnp.mean(center * center, axis=-1, keepdims=True) + epsilon)
    unit = center * inv_dev
    gain_f = gain_full.astype(jnp.float32)
    normed_low = (unit * gain_f + bias_full.astype(jnp.float32)).astype(jnp.bfloat16)
    logits = jnp.dot(normed_low, router_full, preferred_element_type=jnp.float32)
    groups_dev = tok_count // GROUP_SIZE
    local_group = group_ids[0] - ctx_index * groups_dev
    member = (local_group[:, None] == jnp.arange(groups_dev, dtype=jnp.int32)[None, :]).astype(
        jnp.float32
    )
    expo = jnp.exp(logits)
    group_total = jnp.dot(member.T, expo, precision=highest)
    mix_weights = expo / jnp.dot(member, group_total, precision=highest)
    weights_low = mix_weights.astype(jnp.bfloat16)
    mixing = member.astype(jnp.bfloat16).T[:, None, :] * weights_low.T[None, :, :]
    mixing_flat = mixing.reshape(groups_dev * expert_count, tok_count)
    mixed_low = jnp.dot(mixing_flat, normed_low, preferred_element_type=jnp.float32).astype(
        jnp.bfloat16
    )
    mixed_low = mixed_low.reshape(groups_dev, expert_count, width)
    owner_mixed = lax.all_to_all(mixed_low, "fsdp", split_axis=1, concat_axis=0, tiled=True)
    pre, active, owner_out = expert_forward(owner_mixed, w_up, w_down)
    expert_out = lax.all_to_all(owner_out, "fsdp", split_axis=0, concat_axis=1, tiled=True)
    expert_flat = expert_out.reshape(groups_dev * expert_count, width)
    spread = contract_rows(mixing_flat, expert_flat)
    layer_out = hidden + spread
    cot_rows = cotangent[0]
    cot_f = cot_rows.astype(jnp.float32)
    grad_expert = jnp.dot(mixing_flat, cot_rows, preferred_element_type=jnp.float32).astype(
        jnp.bfloat16
    )
    grad_expert = grad_expert.reshape(groups_dev, expert_count, width)
    coef = contract_cols(cot_rows, expert_flat).reshape(tok_count, groups_dev, expert_count)
    grad_mix_spread = jnp.sum(coef * member[:, :, None], axis=1)
    owner_grad = lax.all_to_all(grad_expert, "fsdp", split_axis=1, concat_axis=0, tiled=True)
    grad_up_own, grad_down_own, owner_back = expert_backward(
        owner_mixed, pre, active, owner_grad, w_up, w_down
    )
    grad_mixed = lax.all_to_all(owner_back, "fsdp", split_axis=0, concat_axis=1, tiled=True)
    grad_mixed_flat = grad_mixed.reshape(groups_dev * expert_count, width)
    grad_norm_mix = contract_rows(mixing_flat, grad_mixed_flat)
    grad_mixing = contract_cols(grad_mixed_flat, normed_low).reshape(
        groups_dev, expert_count, tok_count
    )
    grad_mix_mixing = jnp.sum(grad_mixing * member.T[:, None, :], axis=0).T
    grad_mix = grad_mix_spread + grad_mix_mixing
    product = mix_weights * grad_mix
    token_dot = jnp.dot(member, jnp.dot(member.T, product, precision=highest), precision=highest)
    grad_logits = (product - mix_weights * token_dot).astype(jnp.bfloat16)
    grad_router_part = contract_rows(normed_low, grad_logits)
    grad_norm_router = contract_cols(grad_logits, router_full)
    grad_normed = grad_norm_mix + grad_norm_router
    grad_gain_part = jnp.sum(grad_normed * unit, axis=0)
    grad_bias_part = jnp.sum(grad_normed, axis=0)
    scaled = grad_normed * gain_f
    grad_hidden = cot_f + inv_dev * (
        scaled
        - jnp.mean(scaled, axis=-1, keepdims=True)
        - unit * jnp.mean(scaled * unit, axis=-1, keepdims=True)
    )
    grad_branch = grad_hidden.astype(jnp.bfloat16)
    grad_out_part = contract_rows(attended, grad_branch)
    grad_heads = (
        contract_cols(grad_branch, out_full).astype(jnp.bfloat16).reshape(tok_count, HEADS, HEAD)
    )
    delta = jnp.sum(grad_heads.astype(jnp.float32) * accum, axis=-1).T

    def grad_step(grad_query, index):
        probs, key_block, val_block = block_probs(index)
        grad_probs = jnp.einsum(
            "qhd,khd->hqk", grad_heads, val_block, preferred_element_type=jnp.float32
        )
        grad_scores = (probs * (grad_probs - delta[..., None])).astype(jnp.bfloat16)
        grad_query = (
            grad_query
            + jnp.einsum("hqk,khd->qhd", grad_scores, key_block, preferred_element_type=jnp.float32)
            * scale
        )
        grad_key = (
            jnp.einsum("hqk,qhd->khd", grad_scores, query_heads, preferred_element_type=jnp.float32)
            * scale
        )
        grad_val = jnp.einsum(
            "hqk,qhd->khd",
            probs.astype(jnp.bfloat16),
            grad_heads,
            preferred_element_type=jnp.float32,
        )
        return (grad_query, (grad_key, grad_val))

    grad_query, (grad_keys, grad_vals) = lax.scan(
        grad_step, jnp.zeros((tok_count, HEADS, HEAD), jnp.float32), block_ids
    )
    grad_key_own, grad_val_own = (
        lax.psum_scatter(
            grad_keys.reshape(full_rows, width), "ctx", scatter_dimension=0, tiled=True
        ),
        lax.psum_scatter(
            grad_vals.reshape(full_rows, width), "ctx", scatter_dimension=0, tiled=True
        ),
    )
    grad_qkv_low = jnp.concatenate(
        [grad_query.reshape(tok_count, width), grad_key_own, grad_val_own], axis=1
    ).astype(jnp.bfloat16)
    grad_qkv_part = contract_rows(tok_rows, grad_qkv_low)
    grad_tokens = grad_hidden + contract_cols(grad_qkv_low, qkv_full)
    dense = (
        lax.psum_scatter(grad_qkv_part, "fsdp", scatter_dimension=0, tiled=True),
        lax.psum_scatter(grad_out_part, "fsdp", scatter_dimension=0, tiled=True),
        lax.psum_scatter(grad_router_part, "fsdp", scatter_dimension=0, tiled=True),
        lax.psum_scatter(grad_gain_part, "fsdp", scatter_dimension=0, tiled=True),
        lax.psum_scatter(grad_bias_part, "fsdp", scatter_dimension=0, tiled=True),
    )
    totals = lax.psum(
        (dense[0], dense[1], dense[2], dense[3], dense[4], grad_up_own, grad_down_own), "ctx"
    )
    return (
        layer_out[None],
        grad_tokens[None],
        totals[0],
        totals[1],
        totals[2],
        totals[3],
        totals[4],
        totals[5],
        totals[6],
    )


def cost(microseconds):
    return pl.CostEstimate(flops=int(microseconds * 1.15e9), bytes_accessed=1 << 20, transcendentals=0)


LOG2E = 1.4426950408889634
HIDE = -1e30
RUN = 1024
HALF = 512
VMEM = pl.BlockSpec(memory_space=pltpu.VMEM)
SMEM = pl.BlockSpec(memory_space=pltpu.SMEM)
ANY = pl.BlockSpec(memory_space=pl.ANY)
LIMIT = 60 << 20


def dot_nn(left, right):
    return lax.dot_general(left, right, (((1,), (0,)), ((), ())), preferred_element_type=jnp.float32)


def dot_nt(left, right):
    return lax.dot_general(left, right, (((1,), (1,)), ((), ())), preferred_element_type=jnp.float32)


def dot_tn(left, right):
    return lax.dot_general(left, right, (((0,), (0,)), ((), ())), preferred_element_type=jnp.float32)


def split3(value):
    one = value.astype(jnp.bfloat16)
    rest = value - one.astype(jnp.float32)
    two = rest.astype(jnp.bfloat16)
    three = (rest - two.astype(jnp.float32)).astype(jnp.bfloat16)
    return one, two, three


def span(index, size, width=None):
    return pl.ds(pl.multiple_of(index * size, size), size if width is None else width)


MESH = pl.DeviceIdType.MESH


def flip(index, bit):
    return index + bit - 2 * bit * lax.rem(index // bit, 2)


def meet(devices):
    barrier = pltpu.get_barrier_semaphore()
    for device in devices:
        pl.semaphore_signal(barrier, inc=1, device_id=device, device_id_type=MESH)
    pl.semaphore_wait(barrier, len(devices))


def push(src, dst, send_sem, recv_sem, device):
    return pltpu.make_async_remote_copy(
        src_ref=src, dst_ref=dst, send_sem=send_sem, recv_sem=recv_sem, device_id=device, device_id_type=MESH
    )


def norm_parts(hidden):
    center = hidden - jnp.mean(hidden, axis=-1, keepdims=True)
    inv_dev = lax.rsqrt(jnp.mean(center * center, axis=-1, keepdims=True) + epsilon)
    return center * inv_dev, inv_dev


def gelu_parts(value):
    square = value * value
    tangent = jnp.tanh(value * (square * (gelu_coef * gelu_cubic) + gelu_coef))
    half = 0.5 * tangent + 0.5
    rise = value * (square * (3.0 * gelu_coef * gelu_cubic) + gelu_coef)
    return value * half, half + half * (1.0 - tangent) * rise


def boundaries(seg_ref, lane):
    segs = seg_ref[...]
    begin = jnp.zeros(lane.shape, jnp.int32)
    end = jnp.zeros(lane.shape, jnp.int32)
    for c in range(1, 10):
        total = jnp.sum((segs < c).astype(jnp.int32), axis=1, keepdims=True)
        begin = jnp.where(lane == HEAD - 1 + c, total, begin)
        end = jnp.where(lane == HEAD - 2 + c, total, end)
    return begin, jnp.where(lane == HEAD + 8, 0, end)


def layer_body(
    experts, groups, blocks, table_ref, gid_ref, seg_ref, tok_ref, cot_ref, wq_ref, wo_ref, router_ref, gain_ref, bias_ref, up_ref, down_ref,
    gq_ref, out_ref, sums_ref, layer_ref, gtok_ref, act_ref, gpre_ref, all_ref, toks_ref,
    tok, cot, head_buf, pack_buf, heads, wo, pack, zparts, att_send, att, msend, zin, bsend, bin_, up, down, qf, kf, vf, stat, held, late_held,
    ghead_out, ghead, wide_out, ghidden, dof, qt, dot, dk_acc, dv_acc, head_acc, send, landing, weight, zsend, zone, total, totals,
    out_mine, out_zone, out_sum, out_part, out_own, out_all,
    load_sem, own_sem, t_send, t_recv, d_recv, n_send, n_recv, y_send, y_recv, a_send, a_recv, m_send, m_recv, b_send, b_recv,
    h_send, h_recv, s_send, s_recv, z_send, z_recv, c_send, c_recv, o_send, o_recv, g_send, g_recv, r_send, r_recv, w_send, w_recv,
    v_send, v_recv,
):
    me, z = lax.axis_index("ctx"), lax.axis_index("fsdp")
    count, block_len = blocks // 2, tok_ref.shape[0] // 2
    own_rows, width = tok_ref.shape
    owners, own_experts, ffn = msend.shape[0], up_ref.shape[0], up_ref.shape[2]
    flat, per = experts * groups, experts * groups // owners
    rows = blocks * block_len
    runs = rows // RUN
    low = jnp.bfloat16
    dq_acc, qk, dv_rows, sorted_dv = stat, qf, vf, ghead_out

    def start(copies):
        for copy in copies:
            copy.start()
        return copies

    def wait(copies):
        for copy in copies:
            copy.wait()

    loads = []
    for e in range(own_experts):
        loads += [pltpu.make_async_copy(up_ref.at[e], up.at[e], load_sem.at[2 * e])]
        loads += [pltpu.make_async_copy(down_ref.at[e], down.at[e], load_sem.at[2 * e + 1])]
    start(loads)

    def mask(condition):
        return jnp.broadcast_to(jnp.where(condition, 1.0, 0.0), (1, 2 * HEAD))

    def hold_masks(c=None, j=None):
        pairs = [(c, i) if j is None else (i, j) for i in range(count)]
        return [mask(jnp.minimum(table_ref[2 * c], table_ref[2 * c + 1]) == j).astype(low) for c, j in pairs]

    in_order = mask(table_ref[2 * me] < table_ref[2 * me + 1])[:, :1]

    def blend(masks, values):
        out = None
        for weigh, value in zip(masks, values):
            out = weigh * value if out is None else out + weigh * value
        return out

    def ordered(first, second, weigh):
        return weigh * first + (1 - weigh) * second, weigh * second + (1 - weigh) * first

    tok[:block_len, :], tok[block_len:, :] = ordered(tok_ref[:block_len, :], tok_ref[block_len:, :], in_order.astype(low))
    cot[:block_len, :], cot[block_len:, :] = ordered(cot_ref[:block_len, :], cot_ref[block_len:, :], in_order.astype(low))

    sib, xn, yn, diag = flip(me, 1), flip(me, 2), flip(me, 4), flip(flip(me, 2), 4)
    same_core = [xn, yn, diag]
    z_peers = [(me, lax.rem(z + k, owners)) for k in range(1, owners)]
    c_peers = [(jnp.bitwise_xor(me, k), z) for k in range(1, count)]
    meet(z_peers + c_peers)

    piece = block_len // 2
    per_slot = RUN // block_len

    def place(device, half):
        return 2 * half + device // per_slot, lax.rem(device, per_slot) * block_len

    def there(device, half, k):
        slot, at = place(device, half)
        return held.at[slot, pl.ds(pl.multiple_of(at + k * piece, piece), piece)]

    gone = []

    def go(copies):
        gone.extend(start(copies))

    def here(half, k):
        return tok.at[pl.ds(half * block_len + k * piece, piece)]

    def launch(half):
        slot, at = place(me, half)
        held[slot, pl.ds(pl.multiple_of(at, block_len), block_len), :] = tok[half * block_len:(half + 1) * block_len, :]
        for k in (0, 1):
            go([push(here(half, k), there(me, half, k), t_send.at[half, 0, k], t_recv.at[half, 0, k], (xn, z))])
            go([push(here(half, 1 - k), there(me, half, 1 - k), t_send.at[half, 1, 1 - k], t_recv.at[half, 1, 1 - k], (yn, z))])

    def launch_near(half):
        for k in (0, 1):
            go([push(here(half, k), there(me, half, k), n_send.at[half, 0, k], n_recv.at[half, 0, k], (sib, z))])

    def arrived(device, half, k, sem):
        push(there(device, half, k), there(device, half, k), t_send.at[half, 0, 0], sem, (sib, z)).wait_recv()

    def relay(device, half, k, i):
        block = there(device, half, k)
        go([push(block, block, n_send.at[half, i, k], n_recv.at[half, i, k], (sib, z))])

    def forward(half):
        for device, k, i, to in ((xn, 0, 0, yn), (yn, 1, 1, xn)):
            arrived(device, half, k, t_recv.at[half, i, k])
            block = there(device, half, k)
            go([push(block, block, t_send.at[half, 2, k], d_recv.at[half, k], (to, z))])
            relay(device, half, k, i + 1)

    def settle(half):
        arrived(xn, half, 1, t_recv.at[half, 0, 1])
        relay(xn, half, 1, 1)
        arrived(yn, half, 0, t_recv.at[half, 1, 0])
        relay(yn, half, 0, 2)
        for k in (0, 1):
            arrived(diag, half, k, d_recv.at[half, k])
            relay(diag, half, k, 3)
        for k in (0, 1):
            for i, device in enumerate((sib, flip(xn, 1), flip(yn, 1), flip(diag, 1))):
                arrived(device, half, k, n_recv.at[half, i, k])

    launch(0)

    shared = []

    def share(i, shard, whole):
        whole[z] = shard[...]
        shared.append(start([push(shard, whole.at[z], y_send.at[i, k], y_recv.at[i, k], d) for k, d in enumerate(z_peers)]))

    for h in range(count):
        @pl.when(me == h)
        def _():
            cols = [wq_ref[:, width * kind + HEAD * h:width * kind + HEAD * (h + 1)] for kind in range(3)]
            head_buf[...] = jnp.concatenate(cols, axis=1)

    share(0, head_buf, heads)
    launch_near(0)
    parts = [router_ref[...].astype(jnp.float32), gain_ref[...].astype(jnp.float32), bias_ref[...].astype(jnp.float32)]
    parts.append(jnp.zeros((pack_buf.shape[0] - experts - 2, pack_buf.shape[1]), jnp.float32))
    pack_buf[...] = jnp.concatenate(parts, axis=0).astype(low)
    share(1, pack_buf, pack)
    share(2, wo_ref, wo)
    depth = wq_ref.shape[0] // count
    share(3, wq_ref.at[pl.ds(pl.multiple_of(me * depth, depth), depth)], zparts)

    lane = lax.broadcasted_iota(jnp.int32, (1, 2 * HEAD), 1)
    begin, end = boundaries(seg_ref, lane)
    is_flag = (lane >= HEAD) & (lane < HEAD + 8)
    is_one = (lane >= HEAD + 8) & (lane < HEAD + 11)
    ones_v = ((lane >= HEAD) & (lane < HEAD + 3)).astype(jnp.float32)
    scale = HEAD ** (-0.5)

    def projected(half, device):
        at = device % per_slot * block_len
        lanes = device // per_slot * 4 * HEAD
        return held.at[4 + half, at:at + block_len, lanes:lanes + 4 * HEAD]

    def project(half, head_weight):
        @pl.loop(0, count)
        def _(device):
            slot, at = place(device, half)
            rows_here = held[slot, pl.ds(pl.multiple_of(at, block_len), block_len), :]
            slot, at = 4 + half, pl.ds(pl.multiple_of(at, block_len), block_len)
            to = pl.ds(pl.multiple_of(device // per_slot * 4 * HEAD, 4 * HEAD), 4 * HEAD)
            held[slot, at, to] = dot_nn(rows_here, head_weight).astype(low)

        @pl.loop(0, count)
        def _(j):
            s = j if half == 0 else blocks - 1 - j
            masks = hold_masks(j=j)
            both = blend(masks, [projected(half, c)[:, :2 * HEAD] for c in range(count)]).astype(jnp.float32)
            value = blend(masks, [projected(half, c)[:, 2 * HEAD:] for c in range(count)]).astype(jnp.float32)
            spot = lax.broadcasted_iota(jnp.int32, (block_len, 2 * HEAD), 0) + s * block_len
            mine = (spot >= begin) & (spot < end)
            at = span(s, block_len)
            flag_q = jnp.where(is_flag & jnp.logical_not(mine), 1.0, 0.0)
            flag_k = jnp.where(mine, HIDE, jnp.where(is_one, 1.0, 0.0))
            qf[at, :] = jnp.where(lane < HEAD, both, flag_q).astype(low)
            kf[at, :] = jnp.where(lane < HEAD, pltpu.roll(both, HEAD, 1), flag_k).astype(low)
            vf[at, :] = (value + ones_v).astype(low)
            dot[:, at] = value.T.astype(low)[:HEAD]

    lower = lax.broadcasted_iota(jnp.int32, (HALF, HALF), 0) <= lax.broadcasted_iota(jnp.int32, (HALF, HALF), 1)

    def query_run(run):
        def tile(state, q_at, k_at, size, diagonal):
            scores = dot_nt(kf[k_at, :], qf[q_at, :]) * (scale * LOG2E)
            if diagonal:
                scores = jnp.where(lower, scores, HIDE)
            top, acc = state
            new_top = jnp.maximum(top, jnp.max(scores, axis=0, keepdims=True))
            probs = jnp.exp2(scores - new_top).astype(low)
            values = jnp.concatenate([dot[:, k_at], jnp.ones((HEAD, size), low)], axis=0)
            return new_top, acc * jnp.exp2(top - new_top) + dot_nn(values, probs)

        begin = (jnp.full((1, RUN), HIDE, jnp.float32), jnp.zeros((2 * HEAD, RUN), jnp.float32))
        def both_halves(n, state):
            for part in range(2):
                state = tile(state, span(run, RUN), span(2 * n + part, HALF), HALF, False)
            return state

        whole = lax.fori_loop(0, run, both_halves, begin)
        early, late = span(2 * run, HALF), span(2 * run + 1, HALF)
        first = tile([part[:, :HALF] for part in whole], early, early, HALF, True)
        second = tile([part[:, HALF:] for part in whole], late, early, HALF, False)
        second = tile(second, late, late, HALF, True)
        for at, (top, acc) in ((early, first), (late, second)):
            sums = acc[HEAD:]
            result = jnp.concatenate([acc[:HEAD] / sums, top + jnp.log2(sums)], axis=0).T
            stat[at, :] = result
            one, two, three = split3(result * (-1.0 / (scale * LOG2E)))
            old = qf[at, :]
            old = jnp.where(lane == HEAD + 8, one, old)
            old = jnp.where(lane == HEAD + 9, two, old)
            qf[at, :] = jnp.where(lane == HEAD + 10, three, old)

    def send_attended(half):
        mid = block_len // 2
        ats = [slice(s * block_len, (s + 1) * block_len) for s in (range(count) if half == 0 else range(blocks - 1, count - 1, -1))]

        @pl.loop(0, count)
        def _(c):
            block = blend(hold_masks(c=c), [stat[at, :].astype(low) for at in ats])
            att_send[half, c] = jnp.concatenate([block[:mid, :HEAD], block[mid:, :HEAD]], axis=1)
        att[half, me] = att_send[half, me]
        return start([
            push(att_send.at[half, d[0]], att.at[half, me], a_send.at[half, k], a_recv.at[half, k], d) for k, d in enumerate(c_peers)
        ])

    forward(0)
    settle(0)
    launch(1)
    launch_near(1)
    wait(shared[0])
    head_weight = heads[...].reshape(width, 3 * HEAD)
    head_weight = jnp.concatenate([head_weight, jnp.zeros((width, HEAD), low)], axis=1)
    project(0, head_weight)

    @pl.loop(0, 1)
    def _(run):
        query_run(run)

    forward(1)

    @pl.loop(1, runs // 2)
    def _(run):
        query_run(run)

    swap = send_attended(0)
    settle(1)
    saves = start([pltpu.make_async_copy(held.at[i], toks_ref.at[i], own_sem.at[3 + i]) for i in range(rows // RUN)])
    project(1, head_weight)

    @pl.loop(runs // 2, runs)
    def _(run):
        query_run(run)

    swap += send_attended(1)
    for copy in gone:
        copy.wait_send()
    wait(shared[1] + shared[2] + shared[3])

    first_diagonal = runs * (runs - 1)

    def slot_of(run, index, part):
        return run * (2 * runs - 1 - run) + 2 * (index - run - 1) + part

    def probabilities(q_at, k_at, visible):
        scores = dot_nt(qf[q_at, :], kf[k_at, :]) * (scale * LOG2E)
        if visible is not None:
            scores = jnp.where(visible, scores, HIDE)
        return jnp.exp2(scores).astype(low)

    def hold_diagonal():
        early = lax.broadcasted_iota(jnp.int32, (RUN, HALF), 1) <= lax.broadcasted_iota(jnp.int32, (RUN, HALF), 0)
        late = lax.broadcasted_iota(jnp.int32, (HALF, HALF), 1) <= lax.broadcasted_iota(jnp.int32, (HALF, HALF), 0)

        @pl.loop(0, runs)
        def _(run):
            held[first_diagonal + run] = probabilities(span(run, RUN), span(2 * run, HALF), early)
            late_held[run] = probabilities(span(2 * run + 1, HALF), span(2 * run + 1, HALF), late)

    def hold(run):
        @pl.loop(run + 1, runs)
        def _(index):
            for part in range(2):
                held[slot_of(run, index, part)] = probabilities(span(index, RUN), span(2 * run + part, HALF), None)

    hold_diagonal()

    @pl.loop(1, runs - 1)
    def _(run):
        hold(run)

    wait(swap)
    weights = start([push(zparts, weight.at[:, me], w_send.at[k], w_recv.at[k], (d, z)) for k, d in enumerate(same_core)])
    shares = start([push(zparts, weight.at[:, me], v_send.at[3], v_recv.at[3], (sib, z))])
    weight[:, me] = zparts[...]
    quarters = [
        jnp.concatenate([att[half, h, :, HEAD * p:HEAD * (p + 1)] for h in range(count)], axis=1) for half in range(2) for p in range(2)
    ]
    attended = jnp.concatenate(quarters, axis=0)
    out_weight = wo[...].reshape(width, width)
    hidden = tok[...].astype(jnp.float32) + dot_nn(attended, out_weight)
    unit, inv_dev = norm_parts(hidden)
    small_in = jnp.concatenate([pack[k] for k in range(owners)], axis=1)
    gain, bias = small_in[experts:experts + 1].astype(jnp.float32), small_in[experts + 1:experts + 2].astype(jnp.float32)
    normed = (unit * gain + bias).astype(low)
    expo = jnp.exp(dot_nt(small_in, normed)[:experts])
    expo = jnp.broadcast_to(expo[:, None, :], (experts, groups, own_rows)).reshape(flat, own_rows)
    gids = lax.rem(gid_ref[...], groups).astype(jnp.float32)
    gids = jnp.concatenate(ordered(gids[:, :block_len], gids[:, block_len:], in_order), axis=1)
    member = lax.rem(lax.broadcasted_iota(jnp.int32, (flat, 1), 0), groups).astype(jnp.float32) == gids
    expo = jnp.where(member, expo, 0.0)
    mix = expo / jnp.sum(expo, axis=1, keepdims=True)
    mix_low = mix.astype(low)

    def zone_rows(owner, kind):
        return pl.ds(pl.multiple_of((2 * owner + kind) * per, per), per)

    def to_owners(kind, value):
        msend[:, kind] = value.astype(low).reshape(owners, per, width)
        zin[zone_rows(z, kind), :] = msend[z, kind]
        return start([
            push(msend.at[d[1], kind], zin.at[zone_rows(z, kind)], m_send.at[kind, k], m_recv.at[kind, k], d) for k, d in enumerate(z_peers)
        ])

    mixed_copies = to_owners(0, dot_nn(mix_low, normed))
    grad_experts = dot_nn(mix_low, cot[...])
    wait(loads)
    wait(mixed_copies)
    grad_copies = to_owners(1, grad_experts)

    def from_sources(kind, e):
        lows_ = [(2 * owner + kind) * per + e * groups for owner in range(owners)]
        return jnp.concatenate([zin[at:at + groups, :] for at in lows_], axis=0)

    def to_sources(kind, e, value):
        bsend[:, kind, e * groups:(e + 1) * groups, :] = value.astype(low).reshape(owners, groups, width)

    def send_back(kind):
        bin_[z, kind] = bsend[z, kind]
        return start([
            push(bsend.at[d[1], kind], bin_.at[z, kind], b_send.at[kind, k], b_recv.at[kind, k], d) for k, d in enumerate(z_peers)
        ])

    slopes = []
    for e in range(own_experts):
        active, slope = gelu_parts(dot_nn(from_sources(0, e), up[e]))
        slopes.append(slope)
        to_sources(0, e, dot_nn(active.astype(low), down[e]))
    out_copies = send_back(0)
    wait(grad_copies)
    for e in range(own_experts):
        grad_pre = (dot_nt(from_sources(1, e), down[e]) * slopes[e]).astype(low)
        to_sources(1, e, dot_nt(grad_pre, up[e]))
    back_copies = send_back(1)
    wait(out_copies)
    expert_out = bin_[:, 0].reshape(flat, width)
    result = hidden + dot_tn(mix_low, expert_out)
    wide_out[:block_len, :], wide_out[block_len:, :] = ordered(result[:block_len], result[block_len:], in_order)
    layer_copy = start([pltpu.make_async_copy(wide_out, layer_ref, own_sem.at[2])])
    grad_mix = dot_nt(expert_out, cot[...])
    wait(back_copies)
    grad_mixed = bin_[:, 1].reshape(flat, width)
    product = mix * (grad_mix + dot_nt(grad_mixed, normed))
    grad_logits = product - mix * jnp.sum(product, axis=1, keepdims=True)
    grad_logits = jnp.sum(grad_logits.reshape(experts, groups, own_rows), axis=1).astype(low)
    pad = jnp.zeros((small_in.shape[0] - experts, own_rows), low)
    grad_logits = jnp.concatenate([grad_logits, pad], axis=0)
    grad_normed = dot_tn(jnp.concatenate([mix_low, grad_logits], axis=0), jnp.concatenate([grad_mixed, small_in], axis=0))
    scaled = grad_normed * gain
    mean = jnp.mean(scaled, axis=-1, keepdims=True)
    grad_hidden = cot[...].astype(jnp.float32) + inv_dev * (scaled - mean - unit * jnp.mean(scaled * unit, axis=-1, keepdims=True))
    branch = grad_hidden.astype(low)
    grad_heads = dot_nt(branch, out_weight).astype(low)
    for h in range(count):
        at = slice(HEAD * h, HEAD * (h + 1))
        ghead_out[h] = jnp.concatenate([grad_heads[:block_len, at], grad_heads[block_len:, at]], axis=1)
    swap = start([push(ghead_out.at[d[0]], ghead.at[me], h_send.at[k], h_recv.at[k], d) for k, d in enumerate(c_peers)])
    ghead[me] = ghead_out[me]
    ghidden[...] = grad_hidden
    out_mine[...] = dot_tn(attended, branch).astype(low).reshape(out_mine.shape)
    gout_copies = start([push(out_mine.at[d[1]], out_zone.at[z], o_send.at[0, k], o_recv.at[0, k], d) for k, d in enumerate(z_peers)])
    out_zone[z] = out_mine[z]
    small = jnp.concatenate(
        [
            dot_nn(grad_logits, normed)[:experts],
            jnp.sum(grad_normed * unit, axis=0, keepdims=True),
            jnp.sum(grad_normed, axis=0, keepdims=True),
            jnp.zeros((small_in.shape[0] - experts - 2, width), jnp.float32),
        ],
        axis=0,
    )
    lanes = width // owners
    for c in range(owners):
        zsend[c, 3 * HEAD:, :] = small[:, c * lanes:(c + 1) * lanes].astype(low)
    wait(saves)
    hold(0)

    def prepare(s, both):
        at = span(s, block_len)
        grad = jnp.where(lane < HEAD, both, 0.0)
        delta = jnp.sum(grad * stat[at, :], axis=1, keepdims=True)
        one, two, three = split3(jnp.broadcast_to(-delta, grad.shape))
        wide = jnp.where(lane == HEAD, one, grad.astype(low))
        wide = jnp.where(lane == HEAD + 1, two, wide)
        dof[at, :] = jnp.where(lane == HEAD + 2, three, wide)
        turned = jnp.where(lane < HEAD, both, pltpu.roll(qf[at, :].astype(jnp.float32), HEAD, 1)).T.astype(low)
        dot[:, at] = turned[:HEAD]
        qt[:, at] = turned[HEAD:]

    wait(swap)
    gathers = start([push(zin, all_ref.at[me], g_send.at[k], g_recv.at[k], (d, z)) for k, d in enumerate(same_core)])
    relays = start([push(zin, all_ref.at[me], r_send.at[3], r_recv.at[3], (sib, z))])
    own_got = start([pltpu.make_async_copy(zin, all_ref.at[me], own_sem.at[1])])

    @pl.loop(0, count)
    def _(j):
        both = blend(hold_masks(j=j), [ghead[c] for c in range(count)]).astype(jnp.float32)
        prepare(j, both)
        prepare(blocks - 1 - j, pltpu.roll(both, HEAD, 1))

    tok_loads = [
        pltpu.make_async_copy(toks_ref.at[i], held.at[i], own_sem.at[3 + i]) for i in range(rows // RUN)
    ]

    def key_run(run):
        def tile(q_at, k_at, part, probs, first_k, first_q):
            slope = dot_nt(dof[q_at, :], vf[k_at, :])
            grad = (probs.astype(jnp.float32) * slope).astype(low)
            dv = dot_nn(dot[:, q_at], probs)
            dk = dot_nn(qt[:, q_at], grad)
            dq = dot_nn(grad, kf[k_at, :])
            at = slice(part * HALF, (part + 1) * HALF)
            if first_k:
                dv_acc[:, at] = dv
                dk_acc[:, at] = dk
            else:
                dv_acc[:, at] += dv
                dk_acc[:, at] += dk
            if first_q:
                @pl.when(run == 0)
                def _():
                    dq_acc[q_at, :] = dq

                @pl.when(run != 0)
                def _():
                    dq_acc[q_at, :] += dq
            else:
                dq_acc[q_at, :] += dq

        early, late = span(2 * run, HALF), span(2 * run + 1, HALF)
        tile(span(run, RUN), early, 0, held[first_diagonal + run], True, True)
        tile(late, late, 1, late_held[run], True, False)

        @pl.loop(run + 1, runs)
        def _(index):
            for part in range(2):
                tile(span(index, RUN), span(2 * run + part, HALF), part, held[slot_of(run, index, part)], False, part == 0)

        at = span(run, RUN)
        both = jnp.concatenate([dk_acc[...] * scale, dv_acc[...]], axis=0).T
        query = dq_acc[at, :] * scale
        qk[at, :] = jnp.where(lane < HEAD, query, pltpu.roll(both, HEAD, 1)).astype(low)
        dv_rows[at, :] = both.astype(low)

    def send_half(half):
        mid = block_len // 2
        ats = [slice(s * block_len, (s + 1) * block_len) for s in (range(count) if half == 0 else range(blocks - 1, count - 1, -1))]

        @pl.loop(0, count)
        def _(c):
            masks = hold_masks(c=c)
            send[half, c, :block_len, :] = blend(masks, [qk[at, :] for at in ats])
            values = blend(masks, [dv_rows[at, :] for at in ats])
            sorted_dv[c] = values
            values = values[:, HEAD:]
            send[half, c, block_len:, :] = jnp.concatenate([values[:mid], values[mid:]], axis=1)
        landing[half, me] = send[half, me]
        return start([
            push(send.at[half, d[0]], landing.at[half, me], s_send.at[half, k], s_recv.at[half, k], d) for k, d in enumerate(c_peers)
        ])

    def head_weights(half):
        if half == 0:
            head_acc[...] = jnp.zeros_like(head_acc)

        @pl.loop(0, count // 2)
        def _(i):
            first, second = None, None
            for part in range(2):
                c = 2 * i + part
                slot, at = place(c, half)
                here = held[slot, pl.ds(pl.multiple_of(at, block_len), block_len), :]
                one, two = dot_tn(send[half, c, :block_len, :], here), dot_tn(sorted_dv[c], here)
                first, second = (one, two) if first is None else (first + one, second + two)
            head_acc[:2 * HEAD, :] += first
            head_acc[2 * HEAD:, :] += second[HEAD:]

    @pl.loop(0, runs // 2)
    def _(run):
        key_run(run)

        @pl.when(run == 0)
        def _():
            start(tok_loads)

    swaps = send_half(0)
    for k, d in enumerate(same_core):
        gathers[k].wait_recv()
        relays += start([push(all_ref.at[d], all_ref.at[d], r_send.at[k], r_recv.at[k], (sib, z))])
        weights[k].wait_recv()
        shares += start([push(weight.at[:, d], weight.at[:, d], v_send.at[k], v_recv.at[k], (sib, z))])
    wait(gout_copies)
    summed = out_zone[0].astype(jnp.float32)
    for k in range(1, owners):
        summed = summed + out_zone[k].astype(jnp.float32)
    out_sum[...] = summed.astype(low).reshape(out_sum.shape)
    part_copies = start([push(out_sum.at[d[0]], out_part.at[me], o_send.at[1, k], o_recv.at[1, k], d) for k, d in enumerate(c_peers)])
    out_part[me] = out_sum[me]
    wait(tok_loads)
    head_weights(0)

    @pl.loop(runs // 2, runs)
    def _(run):
        key_run(run)

    swaps += send_half(1)
    wait(part_copies)
    summed = out_part[0].astype(jnp.float32)
    for k in range(1, count):
        summed = summed + out_part[k].astype(jnp.float32)
    out_own[...] = summed.astype(low)
    last_copies = start([push(out_own, out_all.at[me], o_send.at[2, k], o_recv.at[2, k], d) for k, d in enumerate(c_peers)])
    out_all[me] = out_own[...]
    wait(own_got + relays)

    mixed_slot = rows // RUN
    share = owners * 2 * per
    mixed_loads = []
    for c in range(count):
        slot, at = divmod(c * share, RUN)
        mixed_loads.append(pltpu.make_async_copy(all_ref.at[c], held.at[mixed_slot + slot, pl.ds(at, share)], own_sem.at[3 + rows // RUN + c]))
    start(mixed_loads)
    head_weights(1)
    for c in range(owners):
        zsend[c, :3 * HEAD, :] = head_acc[:, c * lanes:(c + 1) * lanes].astype(low)
    z_copies = start([push(zsend.at[d[1]], zone.at[z], z_send.at[k], z_recv.at[k], d) for k, d in enumerate(z_peers)])
    zone[z] = zsend[z]
    wait(mixed_loads)
    step = HALF
    chunks = ffn // step
    wide_slot = mixed_slot + count * share // RUN

    def of_expert(kind, e):
        parts = []
        for slot in range(mixed_slot, wide_slot):
            value = held[slot].reshape(RUN // share, owners, 2, own_experts, groups, width)
            parts.append(value[:, :, kind, e].reshape(-1, width))
        return jnp.concatenate(parts, axis=0)

    def expert_part(e):
        mixed, grad_out = of_expert(0, e), of_expert(1, e)
        copies = []

        @pl.loop(0, chunks)
        def _(i):
            at = span(i, step)
            to = span(lax.rem(i, 2), step)
            active, slope = gelu_parts(dot_nn(mixed, up[e, :, at]))
            held[wide_slot + chunks * e + i // 2, to, :] = active.astype(low)
            slot = wide_slot + chunks * e + chunks // 2 + i // 2
            held[slot, to, :] = (dot_nt(grad_out, down[e, at, :]) * slope).astype(low)

        for i in range(chunks):
            slot = wide_slot + chunks * e + i // 2
            at, to = pl.ds(i * step, step), pl.ds(i % 2 * step, step)
            sem = own_sem.at[3 + rows // RUN + count + 2 * (chunks * e + i)]
            copies.append(pltpu.make_async_copy(held.at[slot, to], act_ref.at[e, :, at], sem))
            sem = own_sem.at[4 + rows // RUN + count + 2 * (chunks * e + i)]
            copies.append(pltpu.make_async_copy(held.at[slot + chunks // 2, to], gpre_ref.at[e, :, at], sem))
        return start(copies)

    stores = expert_part(0)
    wait(z_copies)
    summed = zone[0].astype(jnp.float32)
    for k in range(1, owners):
        summed = summed + zone[k].astype(jnp.float32)
    total[...] = summed.astype(low)
    c_copies = start([push(total, totals.at[me], c_send.at[k], c_recv.at[k], d) for k, d in enumerate(c_peers)])
    totals[me] = total[...]
    for e in range(1, own_experts):
        stores += expert_part(e)
    wait(swaps + shares)
    flat_weight = weight[...].reshape(width, -1)
    parts = []
    for half in range(2):
        queries, keys, values = [], [], []
        for h in range(count):
            front, back = landing[half, h, :block_len, :], landing[half, h, block_len:, :]
            queries.append(front[:, :HEAD])
            keys.append(front[:, HEAD:])
            values.append(jnp.concatenate([back[:, :HEAD], back[:, HEAD:]], axis=0))
        parts.append(dot_nt(jnp.concatenate(queries + keys + values, axis=1), flat_weight))
    wait(layer_copy)
    first, second = ghidden[:block_len, :] + parts[0], ghidden[block_len:, :] + parts[1]
    wide_out[:block_len, :], wide_out[block_len:, :] = ordered(first, second, in_order)
    stores += start([pltpu.make_async_copy(wide_out, gtok_ref, own_sem.at[2])])
    wait(last_copies)
    out_ref[...] = out_all[...].astype(jnp.float32).reshape(out_ref.shape)
    wait(c_copies)
    small = None
    turned = []
    for c in range(count):
        turned.append(totals[c, :3 * HEAD, :].astype(jnp.float32).T)
        part = totals[c, 3 * HEAD:, :].astype(jnp.float32)
        small = part if small is None else small + part
    sums_ref[...] = small
    for kind in range(3):
        at = slice(HEAD * kind, HEAD * (kind + 1))
        gq_ref[:, HEAD * count * kind:HEAD * count * (kind + 1)] = jnp.concatenate([part[:, at] for part in turned], axis=1)
    wait(stores)
    for copy in gathers + weights:
        copy.wait_send()


def layer(table, gid_row, segs, tokens, cot, w_qkv, w_out, w_router, ln_gain, ln_bias, w_up, w_down, groups, count, owners):
    own_rows, width = tokens.shape
    experts = w_router.shape[1]
    blocks, block_len = table.shape[0], own_rows // 2
    rows = blocks * block_len
    runs = rows // RUN
    own_experts, _, ffn = w_up.shape
    lanes, wide_qkv = w_qkv.shape
    smalls = 16
    height = 3 * HEAD + smalls
    per = experts * groups // owners
    wide = (own_experts, count * owners * groups, ffn)
    share = (owners * 2 * per, width)
    part = (count, lanes // count, width)
    swap = (2, count, block_len + block_len // 2, 2 * HEAD)
    gout = (owners, lanes, width)
    sent = (owners, 2, per, width)
    attended = (2, count, block_len // 2, 2 * HEAD)
    head_grad = (count, block_len, 2 * HEAD)
    low, full = jnp.bfloat16, jnp.float32
    scratch = [
        (tokens.shape, low), (tokens.shape, low), ((lanes, 3 * HEAD), low), ((smalls, lanes), low), ((owners, lanes, 3 * HEAD), low),
        ((owners,) + w_out.shape, low), ((owners, smalls, lanes), low), ((owners, lanes // count, wide_qkv), low), (attended, low),
        (attended, low), (sent, low), (share, low), (sent, low), (sent, low), (w_up.shape, low), (w_down.shape, low),
        ((rows, 2 * HEAD), low), ((rows, 2 * HEAD), low), ((rows, 2 * HEAD), low), ((rows, 2 * HEAD), full),
        ((runs * runs, RUN, HALF), low), ((runs, HALF, HALF), low), (head_grad, low), (head_grad, low),
        (tokens.shape, full), (tokens.shape, full), ((rows, 2 * HEAD), low), ((HEAD, rows), low), ((HEAD, rows), low),
        ((HEAD, RUN), full), ((HEAD, RUN), full), ((3 * HEAD, width), full), (swap, low), (swap, low),
        ((owners, count, lanes // count, wide_qkv), low), ((owners, height, lanes), low), ((owners, height, lanes), low),
        ((height, lanes), low), ((count, height, lanes), low), (gout, low), (gout, low), (part, low), (part, low), (part[1:], low),
        (part, low),
    ]
    owns = 3 + rows // RUN + count + 2 * own_experts * (ffn // HALF)
    to_z, to_c = owners - 1, count - 1
    sems = [
        (2 * own_experts,), (owns,), (2, 3, 2), (2, 2, 2), (2, 2), (2, 4, 2), (2, 4, 2), (4, to_z), (4, to_z),
        (2, to_c), (2, to_c), (2, to_z), (2, to_z), (2, to_z), (2, to_z), (to_c,), (to_c,), (2, to_c), (2, to_c),
        (to_z,), (to_z,), (to_c,), (to_c,), (3, to_c), (3, to_c), (3,), (3,), (4,), (4,), (3,), (3,), (4,), (4,),
    ]
    return pl.pallas_call(
        functools.partial(layer_body, experts, groups, blocks),
        out_shape=(
            jax.ShapeDtypeStruct((lanes, 3 * width), full),
            jax.ShapeDtypeStruct((lanes, width), full),
            jax.ShapeDtypeStruct((smalls, lanes), full),
            jax.ShapeDtypeStruct(tokens.shape, full),
            jax.ShapeDtypeStruct(tokens.shape, full),
            jax.ShapeDtypeStruct(wide, low),
            jax.ShapeDtypeStruct(wide, low),
            jax.ShapeDtypeStruct((count,) + share, low),
            jax.ShapeDtypeStruct((rows // RUN, RUN, width), low),
        ),
        in_specs=[SMEM] + [VMEM] * 9 + [ANY] * 2,
        out_specs=(VMEM,) * 3 + (ANY,) * 6,
        scratch_shapes=[pltpu.VMEM(shape, dtype) for shape, dtype in scratch] + [pltpu.SemaphoreType.DMA(shape) for shape in sems],
        compiler_params=pltpu.CompilerParams(collective_id=1, has_side_effects=True, vmem_limit_bytes=LIMIT),
        cost_estimate=cost(130),
        name="layer",
    )(table, gid_row, segs, tokens, cot, w_qkv, w_out, w_router.T, ln_gain[None], ln_bias[None], w_up, w_down)


def expert_grad_body(experts, passed, mixed_ref, grad_ref, act_ref, gpre_ref, small_ref, *refs):
    sources, outs = refs[:passed], refs[passed + 5:]
    gup_ref, gdown_ref, router_ref, gain_ref, bias_ref = refs[passed:passed + 5]
    width = gup_ref.shape[1]
    for source, out in zip(sources, outs):
        out[...] = source[...]
    router_ref[...] = small_ref[:experts]
    gain_ref[...] = small_ref[experts:experts + 1]
    bias_ref[...] = small_ref[experts + 1:experts + 2]
    gup_ref[0] = dot_tn(mixed_ref[...].reshape(-1, width), gpre_ref[0])
    gdown_ref[0] = dot_tn(act_ref[0], grad_ref[...].reshape(-1, width))


def expert_grads(gathered, active, grad_pre, small, passed, groups, experts):
    own, rows, ffn = active.shape
    step = 1024
    steps = ffn // step
    sources, width = gathered.shape[0], gathered.shape[3]
    view = gathered.reshape(sources, 2, own, groups, width)
    lanes = small.shape[1]
    full = jnp.float32
    slices = [pl.BlockSpec((x.shape[0] // (own * steps), x.shape[1]), lambda e, f: (e * steps + f, 0)) for x in passed]
    return pl.pallas_call(
        functools.partial(expert_grad_body, experts, len(passed)),
        grid=(own, steps),
        out_shape=[
            jax.ShapeDtypeStruct((own, width, ffn), full), jax.ShapeDtypeStruct((own, ffn, width), full),
            jax.ShapeDtypeStruct((experts, lanes), full), jax.ShapeDtypeStruct((1, lanes), full), jax.ShapeDtypeStruct((1, lanes), full),
        ] + [jax.ShapeDtypeStruct(x.shape, x.dtype) for x in passed],
        in_specs=[
            pl.BlockSpec((sources, 1, 1, groups, width), lambda e, f: (0, 0, e, 0, 0)),
            pl.BlockSpec((sources, 1, 1, groups, width), lambda e, f: (0, 1, e, 0, 0)),
            pl.BlockSpec((1, rows, step), lambda e, f: (e, 0, f)),
            pl.BlockSpec((1, rows, step), lambda e, f: (e, 0, f)),
            pl.BlockSpec(small.shape, lambda e, f: (0, 0)),
        ] + slices,
        out_specs=[
            pl.BlockSpec((1, width, step), lambda e, f: (e, 0, f)), pl.BlockSpec((1, step, width), lambda e, f: (e, f, 0)),
            pl.BlockSpec((experts, lanes), lambda e, f: (0, 0)), pl.BlockSpec((1, lanes), lambda e, f: (0, 0)),
            pl.BlockSpec((1, lanes), lambda e, f: (0, 0)),
        ] + slices,
        compiler_params=pltpu.CompilerParams(vmem_limit_bytes=LIMIT),
        cost_estimate=cost(10),
        name="expert_grads",
    )(view, view, active, grad_pre, small, *passed)


def fast_device(
    tokens, cotangent, block_table, seg_ids, group_ids, w_qkv, w_out, w_router, ln_gain, ln_bias, w_up, w_down
):
    ctx_count, z_count = lax.axis_size("ctx"), lax.axis_size("fsdp")
    tok_rows, cot_rows = tokens[0], cotangent[0]
    rows, width = tok_rows.shape
    experts = w_router.shape[1]
    groups = rows // GROUP_SIZE
    grad_qkv, grad_out, small, layer_out, grad_tokens, active, grad_pre, gathered, unused = layer(
        block_table, group_ids, seg_ids, tok_rows, cot_rows, w_qkv, w_out, w_router, ln_gain, ln_bias, w_up, w_down, groups, ctx_count,
        z_count,
    )
    gathered = gathered.reshape(ctx_count * z_count, 2, experts * groups // z_count, width)
    grad_up, grad_down, grad_router, grad_gain, grad_bias, layer_out, grad_tokens, grad_qkv, grad_out = expert_grads(
        gathered, active, grad_pre, small, [layer_out, grad_tokens, grad_qkv, grad_out], groups, experts
    )
    return (
        layer_out[None],
        grad_tokens[None],
        grad_qkv,
        grad_out,
        grad_router.T,
        grad_gain[0],
        grad_bias[0],
        grad_up,
        grad_down,
    )


def solution(mesh):
    placed = (
        P("fsdp", "ctx", None),
        P("fsdp", "ctx", None),
        P(),
        P("fsdp", None),
        P("fsdp", "ctx"),
        P("fsdp", None),
        P("fsdp", None),
        P("fsdp", None),
        P("fsdp"),
        P("fsdp"),
        P("fsdp", None, None),
        P("fsdp", None, None),
    )
    step = fast_device if mesh.shape["ctx"] == HEADS else on_device
    return jax.shard_map(
        step,
        mesh=mesh,
        in_specs=placed,
        out_specs=(
            P("fsdp", "ctx", None),
            P("fsdp", "ctx", None),
            P("fsdp", None),
            P("fsdp", None),
            P("fsdp", None),
            P("fsdp"),
            P("fsdp"),
            P("fsdp", None, None),
            P("fsdp", None, None),
        ),
        check_vma=False,
    )
```

profile of v0, /device:TPU:0, one launch (start us, length us, event | category | flops | bytes accessed | tf_op | source)
XLA Modules:
  0.0 146.2 jit_solution(14521276154489201161)
XLA Ops:
  0.6 132.0 %layer.1 = (f32[128,1536]{1,0:T(8,128)}, f32[128,512]{1,0:T(8,128)}, f32[16,128]{1,0:T(8,128)}, f32[512,512]{1,0:T(8,128)}, f32[512,512]{1,0:T(8,128)}, /*index=...) custom-call(s32[16]{0:T(128)} %table_ref.1, ...), custom_call_target="tpu_custom_call" | custom-call | flops 149500002304 | bytes 1048576 | tf_op jit(solution)/shard_map/layer/pallas_call | solution.py:1039
  132.7 13.3 %expert_grads.1 = (f32[2,512,2048]{2,1,0:T(8,128)}, f32[2,2048,512]{2,1,0:T(8,128)}, f32[8,128]{1,0:T(8,128)}, f32[1,128]{1,0:T(1,128)}, f32[1,128]{1,0:T(1,128)...) custom-call(bf16[32,2,2,16,512]{4,3,2,1,0:T(8,128)(2,1)} %bitcast.16, ...), custom_call_target="tpu_custom_call" | custom-call | flops 11500000256 | bytes 1048576 | tf_op jit(solution)/shard_map/expert_grads/pallas_call | solution.py:1083
where the time goes:
time: 146 us
  Pallas kernels  145 us (99%)
    pallas_call x1, Pallas kernels, layer(): pl.pallas_call(functools.partial(layer_body, experts, groups, blocks), ou...  132 us
    pallas_call x1, Pallas kernels, expert_grads(): pl.pallas_call(functools.partial(expert_grad_body, experts, len(passed)),...  13.3 us

commit v1 on v0

--- a/solution.py
+++ b/solution.py
@@ -427,14 +427,15 @@
     def ordered(first, second, weigh):
         return weigh * first + (1 - weigh) * second, weigh * second + (1 - weigh) * first
 
-    tok[:block_len, :], tok[block_len:, :] = ordered(tok_ref[:block_len, :], tok_ref[block_len:, :], in_order.astype(low))
-    cot[:block_len, :], cot[block_len:, :] = ordered(cot_ref[:block_len, :], cot_ref[block_len:, :], in_order.astype(low))
-
     sib, xn, yn, diag = flip(me, 1), flip(me, 2), flip(me, 4), flip(flip(me, 2), 4)
     same_core = [xn, yn, diag]
     z_peers = [(me, lax.rem(z + k, owners)) for k in range(1, owners)]
     c_peers = [(jnp.bitwise_xor(me, k), z) for k in range(1, count)]
-    meet(z_peers + c_peers)
+    barrier = pltpu.get_barrier_semaphore()
+    for d in z_peers + c_peers:
+        pl.semaphore_signal(barrier, inc=1, device_id=d, device_id_type=MESH)
+    tok[:block_len, :], tok[block_len:, :] = ordered(tok_ref[:block_len, :], tok_ref[block_len:, :], in_order.astype(low))
+    pl.semaphore_wait(barrier, len(z_peers + c_peers))
 
     piece = block_len // 2
     per_slot = RUN // block_len
@@ -465,31 +466,47 @@
         for k in (0, 1):
             go([push(here(half, k), there(me, half, k), n_send.at[half, 0, k], n_recv.at[half, 0, k], (sib, z))])
 
-    def arrived(device, half, k, sem):
-        push(there(device, half, k), there(device, half, k), t_send.at[half, 0, 0], sem, (sib, z)).wait_recv()
+    def arrival(device, half, k, sem):
+        return push(there(device, half, k), there(device, half, k), t_send.at[half, 0, 0], sem, (sib, z))
 
     def relay(device, half, k, i):
         block = there(device, half, k)
-        go([push(block, block, n_send.at[half, i, k], n_recv.at[half, i, k], (sib, z))])
-
-    def forward(half):
+        return push(block, block, n_send.at[half, i, k], n_recv.at[half, i, k], (sib, z))
+
+    def forward_plan(half):
+        plan = []
         for device, k, i, to in ((xn, 0, 0, yn), (yn, 1, 1, xn)):
-            arrived(device, half, k, t_recv.at[half, i, k])
             block = there(device, half, k)
-            go([push(block, block, t_send.at[half, 2, k], d_recv.at[half, k], (to, z))])
-            relay(device, half, k, i + 1)
-
-    def settle(half):
-        arrived(xn, half, 1, t_recv.at[half, 0, 1])
-        relay(xn, half, 1, 1)
-        arrived(yn, half, 0, t_recv.at[half, 1, 0])
-        relay(yn, half, 0, 2)
-        for k in (0, 1):
-            arrived(diag, half, k, d_recv.at[half, k])
-            relay(diag, half, k, 3)
+            plan.append((
+                push(block, block, t_send.at[half, 0, 0], t_recv.at[half, i, k], (sib, z)),
+                push(block, block, t_send.at[half, 2, k], d_recv.at[half, k], (to, z)),
+                push(block, block, n_send.at[half, i + 1, k], n_recv.at[half, i + 1, k], (sib, z)),
+            ))
+        return plan
+
+    def forward(plan):
+        for came, on, near in plan:
+            came.wait_recv()
+            start([on, near])
+
+    def settle_plan(half):
+        plan = [
+            (arrival(xn, half, 1, t_recv.at[half, 0, 1]), relay(xn, half, 1, 1)),
+            (arrival(yn, half, 0, t_recv.at[half, 1, 0]), relay(yn, half, 0, 2)),
+        ]
+        plan += [(arrival(diag, half, k, d_recv.at[half, k]), relay(diag, half, k, 3)) for k in (0, 1)]
+        near = []
         for k in (0, 1):
             for i, device in enumerate((sib, flip(xn, 1), flip(yn, 1), flip(diag, 1))):
-                arrived(device, half, k, n_recv.at[half, i, k])
+                near.append(arrival(device, half, k, n_recv.at[half, i, k]))
+        return plan, near
+
+    def settle(plan, near):
+        for came, on in plan:
+            came.wait_recv()
+            on.start()
+        for came in near:
+            came.wait_recv()
 
     launch(0)
 
@@ -528,15 +545,11 @@
         return held.at[4 + half, at:at + block_len, lanes:lanes + 4 * HEAD]
 
     def project(half, head_weight):
-        @pl.loop(0, count)
-        def _(device):
-            slot, at = place(device, half)
-            rows_here = held[slot, pl.ds(pl.multiple_of(at, block_len), block_len), :]
-            slot, at = 4 + half, pl.ds(pl.multiple_of(at, block_len), block_len)
-            to = pl.ds(pl.multiple_of(device // per_slot * 4 * HEAD, 4 * HEAD), 4 * HEAD)
-            held[slot, at, to] = dot_nn(rows_here, head_weight).astype(low)
-
-        @pl.loop(0, count)
+        for slot in range(count // per_slot):
+            to = slice(4 * HEAD * slot, 4 * HEAD * (slot + 1))
+            held[4 + half, :, to] = dot_nn(held[2 * half + slot], head_weight).astype(low)
+
+        @pl.loop(0, count, unroll=4)
         def _(j):
             s = j if half == 0 else blocks - 1 - j
             masks = hold_masks(j=j)
@@ -552,13 +565,13 @@
             vf[at, :] = (value + ones_v).astype(low)
             dot[:, at] = value.T.astype(low)[:HEAD]
 
-    lower = lax.broadcasted_iota(jnp.int32, (HALF, HALF), 0) <= lax.broadcasted_iota(jnp.int32, (HALF, HALF), 1)
+    lower = lax.broadcasted_iota(jnp.int32, (HALF, RUN), 0) <= lax.broadcasted_iota(jnp.int32, (HALF, RUN), 1)
 
     def query_run(run):
         def tile(state, q_at, k_at, size, diagonal):
             scores = dot_nt(kf[k_at, :], qf[q_at, :]) * (scale * LOG2E)
             if diagonal:
-                scores = jnp.where(lower, scores, HIDE)
+                scores = jnp.where(lower[:, :scores.shape[1]], scores, HIDE)
             top, acc = state
             new_top = jnp.maximum(top, jnp.max(scores, axis=0, keepdims=True))
             probs = jnp.exp2(scores - new_top).astype(low)
@@ -573,9 +586,9 @@
 
         whole = lax.fori_loop(0, run, both_halves, begin)
         early, late = span(2 * run, HALF), span(2 * run + 1, HALF)
-        first = tile([part[:, :HALF] for part in whole], early, early, HALF, True)
-        second = tile([part[:, HALF:] for part in whole], late, early, HALF, False)
-        second = tile(second, late, late, HALF, True)
+        whole = tile(whole, span(run, RUN), early, HALF, True)
+        first = [part[:, :HALF] for part in whole]
+        second = tile([part[:, HALF:] for part in whole], late, late, HALF, True)
         for at, (top, acc) in ((early, first), (late, second)):
             sums = acc[HEAD:]
             result = jnp.concatenate([acc[:HEAD] / sums, top + jnp.log2(sums)], axis=0).T
@@ -586,21 +599,31 @@
             old = jnp.where(lane == HEAD + 9, two, old)
             qf[at, :] = jnp.where(lane == HEAD + 10, three, old)
 
-    def send_attended(half):
+    def pack_attended(half):
         mid = block_len // 2
         ats = [slice(s * block_len, (s + 1) * block_len) for s in (range(count) if half == 0 else range(blocks - 1, count - 1, -1))]
 
-        @pl.loop(0, count)
+        @pl.loop(0, count, unroll=4)
         def _(c):
             block = blend(hold_masks(c=c), [stat[at, :].astype(low) for at in ats])
             att_send[half, c] = jnp.concatenate([block[:mid, :HEAD], block[mid:, :HEAD]], axis=1)
         att[half, me] = att_send[half, me]
-        return start([
-            push(att_send.at[half, d[0]], att.at[half, me], a_send.at[half, k], a_recv.at[half, k], d) for k, d in enumerate(c_peers)
-        ])
-
-    forward(0)
-    settle(0)
+
+    swaps = [
+        [push(att_send.at[half, d[0]], att.at[half, me], a_send.at[half, k], a_recv.at[half, k], d) for k, d in enumerate(c_peers)]
+        for half in range(2)
+    ]
+    saves = [pltpu.make_async_copy(held.at[i], toks_ref.at[i], own_sem.at[3 + i]) for i in range(rows // RUN)]
+    cot[:block_len, :], cot[block_len:, :] = ordered(cot_ref[:block_len, :], cot_ref[block_len:, :], in_order.astype(low))
+    plans = [forward_plan(half) for half in range(2)]
+    for plan in plans:
+        for came, on, near in plan:
+            gone.extend([on, near])
+    settles = [settle_plan(half) for half in range(2)]
+    for plan, near in settles:
+        gone.extend([on for came, on in plan])
+    forward(plans[0])
+    settle(*settles[0])
     launch(1)
     launch_near(1)
     wait(shared[0])
@@ -608,26 +631,24 @@
     head_weight = jnp.concatenate([head_weight, jnp.zeros((width, HEAD), low)], axis=1)
     project(0, head_weight)
 
-    @pl.loop(0, 1)
+    @pl.loop(0, runs)
     def _(run):
         query_run(run)
 
-    forward(1)
-
-    @pl.loop(1, runs // 2)
-    def _(run):
-        query_run(run)
-
-    swap = send_attended(0)
-    settle(1)
-    saves = start([pltpu.make_async_copy(held.at[i], toks_ref.at[i], own_sem.at[3 + i]) for i in range(rows // RUN)])
-    project(1, head_weight)
-
-    @pl.loop(runs // 2, runs)
-    def _(run):
-        query_run(run)
-
-    swap += send_attended(1)
+        @pl.when(run == 0)
+        def _():
+            forward(plans[1])
+
+        @pl.when(run == runs // 2 - 1)
+        def _():
+            pack_attended(0)
+            start(swaps[0])
+            settle(*settles[1])
+            start(saves)
+            project(1, head_weight)
+
+    pack_attended(1)
+    start(swaps[1])
     for copy in gone:
         copy.wait_send()
     wait(shared[1] + shared[2] + shared[3])
@@ -659,12 +680,7 @@
                 held[slot_of(run, index, part)] = probabilities(span(index, RUN), span(2 * run + part, HALF), None)
 
     hold_diagonal()
-
-    @pl.loop(1, runs - 1)
-    def _(run):
-        hold(run)
-
-    wait(swap)
+    wait(swaps[0] + swaps[1])
     weights = start([push(zparts, weight.at[:, me], w_send.at[k], w_recv.at[k], (d, z)) for k, d in enumerate(same_core)])
     shares = start([push(zparts, weight.at[:, me], v_send.at[3], v_recv.at[3], (sib, z))])
     weight[:, me] = zparts[...]
@@ -700,8 +716,14 @@
     mixed_copies = to_owners(0, dot_nn(mix_low, normed))
     grad_experts = dot_nn(mix_low, cot[...])
     wait(loads)
+    hold(1)
+    grad_copies = to_owners(1, grad_experts)
+
+    @pl.loop(2, runs - 1)
+    def _(run):
+        hold(run)
+
     wait(mixed_copies)
-    grad_copies = to_owners(1, grad_experts)
 
     def from_sources(kind, e):
         lows_ = [(2 * owner + kind) * per + e * groups for owner in range(owners)]
@@ -784,10 +806,10 @@
 
     wait(swap)
     gathers = start([push(zin, all_ref.at[me], g_send.at[k], g_recv.at[k], (d, z)) for k, d in enumerate(same_core)])
-    relays = start([push(zin, all_ref.at[me], r_send.at[3], r_recv.at[3], (sib, z))])
+    own_relay = start([push(zin, all_ref.at[me], r_send.at[3], r_recv.at[3], (sib, z))])
     own_got = start([pltpu.make_async_copy(zin, all_ref.at[me], own_sem.at[1])])
 
-    @pl.loop(0, count)
+    @pl.loop(0, count, unroll=4)
     def _(j):
         both = blend(hold_masks(j=j), [ghead[c] for c in range(count)]).astype(jnp.float32)
         prepare(j, both)
@@ -837,11 +859,11 @@
         qk[at, :] = jnp.where(lane < HEAD, query, pltpu.roll(both, HEAD, 1)).astype(low)
         dv_rows[at, :] = both.astype(low)
 
-    def send_half(half):
+    def pack_half(half):
         mid = block_len // 2
         ats = [slice(s * block_len, (s + 1) * block_len) for s in (range(count) if half == 0 else range(blocks - 1, count - 1, -1))]
 
-        @pl.loop(0, count)
+        @pl.loop(0, count, unroll=4)
         def _(c):
             masks = hold_masks(c=c)
             send[half, c, :block_len, :] = blend(masks, [qk[at, :] for at in ats])
@@ -850,9 +872,14 @@
             values = values[:, HEAD:]
             send[half, c, block_len:, :] = jnp.concatenate([values[:mid], values[mid:]], axis=1)
         landing[half, me] = send[half, me]
-        return start([
-            push(send.at[half, d[0]], landing.at[half, me], s_send.at[half, k], s_recv.at[half, k], d) for k, d in enumerate(c_peers)
-        ])
+
+    swaps = [
+        [push(send.at[half, d[0]], landing.at[half, me], s_send.at[half, k], s_recv.at[half, k], d) for k, d in enumerate(c_peers)]
+        for half in range(2)
+    ]
+    relays = [push(all_ref.at[d], all_ref.at[d], r_send.at[k], r_recv.at[k], (sib, z)) for k, d in enumerate(same_core)]
+    others = [push(weight.at[:, d], weight.at[:, d], v_send.at[k], v_recv.at[k], (sib, z)) for k, d in enumerate(same_core)]
+    part_copies = [push(out_sum.at[d[0]], out_part.at[me], o_send.at[1, k], o_recv.at[1, k], d) for k, d in enumerate(c_peers)]
 
     def head_weights(half):
         if half == 0:
@@ -870,7 +897,7 @@
             head_acc[:2 * HEAD, :] += first
             head_acc[2 * HEAD:, :] += second[HEAD:]
 
-    @pl.loop(0, runs // 2)
+    @pl.loop(0, runs)
     def _(run):
         key_run(run)
 
@@ -878,27 +905,27 @@
         def _():
             start(tok_loads)
 
-    swaps = send_half(0)
-    for k, d in enumerate(same_core):
-        gathers[k].wait_recv()
-        relays += start([push(all_ref.at[d], all_ref.at[d], r_send.at[k], r_recv.at[k], (sib, z))])
-        weights[k].wait_recv()
-        shares += start([push(weight.at[:, d], weight.at[:, d], v_send.at[k], v_recv.at[k], (sib, z))])
-    wait(gout_copies)
-    summed = out_zone[0].astype(jnp.float32)
-    for k in range(1, owners):
-        summed = summed + out_zone[k].astype(jnp.float32)
-    out_sum[...] = summed.astype(low).reshape(out_sum.shape)
-    part_copies = start([push(out_sum.at[d[0]], out_part.at[me], o_send.at[1, k], o_recv.at[1, k], d) for k, d in enumerate(c_peers)])
-    out_part[me] = out_sum[me]
-    wait(tok_loads)
-    head_weights(0)
-
-    @pl.loop(runs // 2, runs)
-    def _(run):
-        key_run(run)
-
-    swaps += send_half(1)
+        @pl.when(run == runs // 2 - 1)
+        def _():
+            pack_half(0)
+            start(swaps[0])
+            for k in range(len(same_core)):
+                gathers[k].wait_recv()
+                relays[k].start()
+                weights[k].wait_recv()
+                others[k].start()
+            wait(gout_copies)
+            summed = out_zone[0].astype(jnp.float32)
+            for k in range(1, owners):
+                summed = summed + out_zone[k].astype(jnp.float32)
+            out_sum[...] = summed.astype(low).reshape(out_sum.shape)
+            start(part_copies)
+            out_part[me] = out_sum[me]
+            wait(tok_loads)
+            head_weights(0)
+
+    pack_half(1)
+    start(swaps[1])
     wait(part_copies)
     summed = out_part[0].astype(jnp.float32)
     for k in range(1, count):
@@ -906,7 +933,7 @@
     out_own[...] = summed.astype(low)
     last_copies = start([push(out_own, out_all.at[me], o_send.at[2, k], o_recv.at[2, k], d) for k, d in enumerate(c_peers)])
     out_all[me] = out_own[...]
-    wait(own_got + relays)
+    wait(own_got + own_relay + relays)
 
     mixed_slot = rows // RUN
     share = owners * 2 * per
@@ -964,7 +991,7 @@
     totals[me] = total[...]
     for e in range(1, own_experts):
         stores += expert_part(e)
-    wait(swaps + shares)
+    wait(swaps[0] + swaps[1] + shares + others)
     flat_weight = weight[...].reshape(width, -1)
     parts = []
     for half in range(2):
@@ -1073,7 +1100,7 @@
 
 def expert_grads(gathered, active, grad_pre, small, passed, groups, experts):
     own, rows, ffn = active.shape
-    step = 1024
+    step = ffn
     steps = ffn // step
     sources, width = gathered.shape[0], gathered.shape[3]
     view = gathered.reshape(sources, 2, own, groups, width)

time: 146 us -> 140 us (0.959)
  Pallas kernels: 145 us -> 139 us
    pallas_call x1, Pallas kernels: 132 us -> 127 us  [layer(): pl.pallas_call(functools.partial(layer_body, experts, groups, blocks), ou...]
where the time goes in v1:
time: 140 us; the launch traced here: 139 us
  Pallas kernels  139 us (99%)
    pallas_call x1, Pallas kernels, layer(): pl.pallas_call(functools.partial(layer_body, experts, groups, blocks), ou...  127 us
    pallas_call x1, Pallas kernels, expert_grads(): pl.pallas_call(functools.partial(expert_grad_body, experts, len(passed)),...  12 us

profile of v1, /device:TPU:0, one launch (start us, length us, event | category | flops | bytes accessed | tf_op | source)
XLA Modules:
  0.0 139.5 jit_solution(8093856227511812048)
XLA Ops:
  0.6 126.6 %layer.1 = (f32[128,1536]{1,0:T(8,128)}, f32[128,512]{1,0:T(8,128)}, f32[16,128]{1,0:T(8,128)}, f32[512,512]{1,0:T(8,128)}, f32[512,512]{1,0:T(8,128)}, /*index=...) custom-call(s32[16]{0:T(128)} %table_ref.1, ...), custom_call_target="tpu_custom_call" | custom-call | flops 149500002304 | bytes 1048576 | tf_op jit(solution)/shard_map/layer/pallas_call | solution.py:1066
  127.3 12.0 %expert_grads.1 = (f32[2,512,2048]{2,1,0:T(8,128)}, f32[2,2048,512]{2,1,0:T(8,128)}, f32[8,128]{1,0:T(8,128)}, f32[1,128]{1,0:T(1,128)}, f32[1,128]{1,0:T(1,128)...) custom-call(bf16[32,2,2,16,512]{4,3,2,1,0:T(8,128)(2,1)} %bitcast.16, ...), custom_call_target="tpu_custom_call" | custom-call | flops 11500000256 | bytes 1048576 | tf_op jit(solution)/shard_map/expert_grads/pallas_call | solution.py:1110

commit v2 on v1

--- a/solution.py
+++ b/solution.py
@@ -549,7 +549,7 @@
             to = slice(4 * HEAD * slot, 4 * HEAD * (slot + 1))
             held[4 + half, :, to] = dot_nn(held[2 * half + slot], head_weight).astype(low)
 
-        @pl.loop(0, count, unroll=4)
+        @pl.loop(0, count, unroll=8)
         def _(j):
             s = j if half == 0 else blocks - 1 - j
             masks = hold_masks(j=j)
@@ -732,29 +732,34 @@
     def to_sources(kind, e, value):
         bsend[:, kind, e * groups:(e + 1) * groups, :] = value.astype(low).reshape(owners, groups, width)
 
-    def send_back(kind):
-        bin_[z, kind] = bsend[z, kind]
+    def send_back(kind, e):
+        at = pl.ds(e * groups, groups)
+        bin_[z, kind, at, :] = bsend[z, kind, at, :]
         return start([
-            push(bsend.at[d[1], kind], bin_.at[z, kind], b_send.at[kind, k], b_recv.at[kind, k], d) for k, d in enumerate(z_peers)
+            push(bsend.at[d[1], kind, at], bin_.at[z, kind, at], b_send.at[kind, e, k], b_recv.at[kind, e, k], d)
+            for k, d in enumerate(z_peers)
         ])
 
+    out_copies, back_copies = [], []
     slopes = []
     for e in range(own_experts):
         active, slope = gelu_parts(dot_nn(from_sources(0, e), up[e]))
         slopes.append(slope)
         to_sources(0, e, dot_nn(active.astype(low), down[e]))
-    out_copies = send_back(0)
+        out_copies += send_back(0, e)
     wait(grad_copies)
     for e in range(own_experts):
         grad_pre = (dot_nt(from_sources(1, e), down[e]) * slopes[e]).astype(low)
         to_sources(1, e, dot_nt(grad_pre, up[e]))
-    back_copies = send_back(1)
+        back_copies += send_back(1, e)
     wait(out_copies)
     expert_out = bin_[:, 0].reshape(flat, width)
     result = hidden + dot_tn(mix_low, expert_out)
     wide_out[:block_len, :], wide_out[block_len:, :] = ordered(result[:block_len], result[block_len:], in_order)
     layer_copy = start([pltpu.make_async_copy(wide_out, layer_ref, own_sem.at[2])])
     grad_mix = dot_nt(expert_out, cot[...])
+    wait(saves)
+    hold(0)
     wait(back_copies)
     grad_mixed = bin_[:, 1].reshape(flat, width)
     product = mix * (grad_mix + dot_nt(grad_mixed, normed))
@@ -789,8 +794,6 @@
     lanes = width // owners
     for c in range(owners):
         zsend[c, 3 * HEAD:, :] = small[:, c * lanes:(c + 1) * lanes].astype(low)
-    wait(saves)
-    hold(0)
 
     def prepare(s, both):
         at = span(s, block_len)
@@ -879,6 +882,7 @@
     ]
     relays = [push(all_ref.at[d], all_ref.at[d], r_send.at[k], r_recv.at[k], (sib, z)) for k, d in enumerate(same_core)]
     others = [push(weight.at[:, d], weight.at[:, d], v_send.at[k], v_recv.at[k], (sib, z)) for k, d in enumerate(same_core)]
+    last_copies = [push(out_own, out_all.at[me], o_send.at[2, k], o_recv.at[2, k], d) for k, d in enumerate(c_peers)]
     part_copies = [push(out_sum.at[d[0]], out_part.at[me], o_send.at[1, k], o_recv.at[1, k], d) for k, d in enumerate(c_peers)]
 
     def head_weights(half):
@@ -907,6 +911,13 @@
 
         @pl.when(run == runs // 2 - 1)
         def _():
+            wait(gout_copies)
+            summed = out_zone[0].astype(jnp.float32)
+            for k in range(1, owners):
+                summed = summed + out_zone[k].astype(jnp.float32)
+            out_sum[...] = summed.astype(low).reshape(out_sum.shape)
+            start(part_copies)
+            out_part[me] = out_sum[me]
             pack_half(0)
             start(swaps[0])
             for k in range(len(same_core)):
@@ -914,25 +925,21 @@
                 relays[k].start()
                 weights[k].wait_recv()
                 others[k].start()
-            wait(gout_copies)
-            summed = out_zone[0].astype(jnp.float32)
-            for k in range(1, owners):
-                summed = summed + out_zone[k].astype(jnp.float32)
-            out_sum[...] = summed.astype(low).reshape(out_sum.shape)
-            start(part_copies)
-            out_part[me] = out_sum[me]
             wait(tok_loads)
             head_weights(0)
 
+        @pl.when(run == runs // 2)
+        def _():
+            wait(part_copies)
+            summed = out_part[0].astype(jnp.float32)
+            for k in range(1, count):
+                summed = summed + out_part[k].astype(jnp.float32)
+            out_own[...] = summed.astype(low)
+            start(last_copies)
+            out_all[me] = out_own[...]
+
     pack_half(1)
     start(swaps[1])
-    wait(part_copies)
-    summed = out_part[0].astype(jnp.float32)
-    for k in range(1, count):
-        summed = summed + out_part[k].astype(jnp.float32)
-    out_own[...] = summed.astype(low)
-    last_copies = start([push(out_own, out_all.at[me], o_send.at[2, k], o_recv.at[2, k], d) for k, d in enumerate(c_peers)])
-    out_all[me] = out_own[...]
     wait(own_got + own_relay + relays)
 
     mixed_slot = rows // RUN
@@ -963,7 +970,7 @@
         mixed, grad_out = of_expert(0, e), of_expert(1, e)
         copies = []
 
-        @pl.loop(0, chunks)
+        @pl.loop(0, chunks, unroll=2)
         def _(i):
             at = span(i, step)
             to = span(lax.rem(i, 2), step)
@@ -1060,7 +1067,7 @@
     to_z, to_c = owners - 1, count - 1
     sems = [
         (2 * own_experts,), (owns,), (2, 3, 2), (2, 2, 2), (2, 2), (2, 4, 2), (2, 4, 2), (4, to_z), (4, to_z),
-        (2, to_c), (2, to_c), (2, to_z), (2, to_z), (2, to_z), (2, to_z), (to_c,), (to_c,), (2, to_c), (2, to_c),
+        (2, to_c), (2, to_c), (2, to_z), (2, to_z), (2, own_experts, to_z), (2, own_experts, to_z), (to_c,), (to_c,), (2, to_c), (2, to_c),
         (to_z,), (to_z,), (to_c,), (to_c,), (3, to_c), (3, to_c), (3,), (3,), (4,), (4,), (3,), (3,), (4,), (4,),
     ]
     return pl.pallas_call(

time: 140 us -> 138 us (0.986)
  Pallas kernels: 139 us -> 137 us
    pallas_call x1, Pallas kernels: 127 us -> 125 us  [layer(): pl.pallas_call(functools.partial(layer_body, experts, groups, blocks), ou...]
where the time goes in v2:
time: 138 us
  Pallas kernels  137 us (99%)
    pallas_call x1, Pallas kernels, layer(): pl.pallas_call(functools.partial(layer_body, experts, groups, blocks), ou...  125 us
    pallas_call x1, Pallas kernels, expert_grads(): pl.pallas_call(functools.partial(expert_grad_body, experts, len(passed)),...  12 us

profile of v2, /device:TPU:0, one launch (start us, length us, event | category | flops | bytes accessed | tf_op | source)
XLA Modules:
  0.0 138.0 jit_solution(6440450003453154598)
XLA Ops:
  0.6 125.1 %layer.1 = (f32[128,1536]{1,0:T(8,128)}, f32[128,512]{1,0:T(8,128)}, f32[16,128]{1,0:T(8,128)}, f32[512,512]{1,0:T(8,128)}, f32[512,512]{1,0:T(8,128)}, /*index=...) custom-call(s32[16]{0:T(128)} %table_ref.1, ...), custom_call_target="tpu_custom_call" | custom-call | flops 149500002304 | bytes 1048576 | tf_op jit(solution)/shard_map/layer/pallas_call | solution.py:1073
  125.8 12.0 %expert_grads.1 = (f32[2,512,2048]{2,1,0:T(8,128)}, f32[2,2048,512]{2,1,0:T(8,128)}, f32[8,128]{1,0:T(8,128)}, f32[1,128]{1,0:T(1,128)}, f32[1,128]{1,0:T(1,128)...) custom-call(bf16[32,2,2,16,512]{4,3,2,1,0:T(8,128)(2,1)} %bitcast.16, ...), custom_call_target="tpu_custom_call" | custom-call | flops 11500000256 | bytes 1048576 | tf_op jit(solution)/shard_map/expert_grads/pallas_call | solution.py:1117

commit v3 on v2

--- a/solution.py
+++ b/solution.py
@@ -940,6 +940,11 @@
 
     pack_half(1)
     start(swaps[1])
+    head_weights(1)
+    for c in range(owners):
+        zsend[c, :3 * HEAD, :] = head_acc[:, c * lanes:(c + 1) * lanes].astype(low)
+    z_copies = start([push(zsend.at[d[1]], zone.at[z], z_send.at[k], z_recv.at[k], d) for k, d in enumerate(z_peers)])
+    zone[z] = zsend[z]
     wait(own_got + own_relay + relays)
 
     mixed_slot = rows // RUN
@@ -949,11 +954,6 @@
         slot, at = divmod(c * share, RUN)
         mixed_loads.append(pltpu.make_async_copy(all_ref.at[c], held.at[mixed_slot + slot, pl.ds(at, share)], own_sem.at[3 + rows // RUN + c]))
     start(mixed_loads)
-    head_weights(1)
-    for c in range(owners):
-        zsend[c, :3 * HEAD, :] = head_acc[:, c * lanes:(c + 1) * lanes].astype(low)
-    z_copies = start([push(zsend.at[d[1]], zone.at[z], z_send.at[k], z_recv.at[k], d) for k, d in enumerate(z_peers)])
-    zone[z] = zsend[z]
     wait(mixed_loads)
     step = HALF
     chunks = ffn // step
@@ -1014,7 +1014,7 @@
     wide_out[:block_len, :], wide_out[block_len:, :] = ordered(first, second, in_order)
     stores += start([pltpu.make_async_copy(wide_out, gtok_ref, own_sem.at[2])])
     wait(last_copies)
-    out_ref[...] = out_all[...].astype(jnp.float32).reshape(out_ref.shape)
+    out_ref[...] = out_all[...].reshape(out_ref.shape)
     wait(c_copies)
     small = None
     turned = []
@@ -1025,7 +1025,7 @@
     sums_ref[...] = small
     for kind in range(3):
         at = slice(HEAD * kind, HEAD * (kind + 1))
-        gq_ref[:, HEAD * count * kind:HEAD * count * (kind + 1)] = jnp.concatenate([part[:, at] for part in turned], axis=1)
+        gq_ref[:, HEAD * count * kind:HEAD * count * (kind + 1)] = jnp.concatenate([part[:, at] for part in turned], axis=1).astype(low)
     wait(stores)
     for copy in gathers + weights:
         copy.wait_send()
@@ -1073,8 +1073,8 @@
     return pl.pallas_call(
         functools.partial(layer_body, experts, groups, blocks),
         out_shape=(
-            jax.ShapeDtypeStruct((lanes, 3 * width), full),
-            jax.ShapeDtypeStruct((lanes, width), full),
+            jax.ShapeDtypeStruct((lanes, 3 * width), low),
+            jax.ShapeDtypeStruct((lanes, width), low),
             jax.ShapeDtypeStruct((smalls, lanes), full),
             jax.ShapeDtypeStruct(tokens.shape, full),
             jax.ShapeDtypeStruct(tokens.shape, full),
@@ -1097,7 +1097,7 @@
     gup_ref, gdown_ref, router_ref, gain_ref, bias_ref = refs[passed:passed + 5]
     width = gup_ref.shape[1]
     for source, out in zip(sources, outs):
-        out[...] = source[...]
+        out[...] = source[...].astype(out.dtype)
     router_ref[...] = small_ref[:experts]
     gain_ref[...] = small_ref[experts:experts + 1]
     bias_ref[...] = small_ref[experts + 1:experts + 2]
@@ -1120,7 +1120,7 @@
         out_shape=[
             jax.ShapeDtypeStruct((own, width, ffn), full), jax.ShapeDtypeStruct((own, ffn, width), full),
             jax.ShapeDtypeStruct((experts, lanes), full), jax.ShapeDtypeStruct((1, lanes), full), jax.ShapeDtypeStruct((1, lanes), full),
-        ] + [jax.ShapeDtypeStruct(x.shape, x.dtype) for x in passed],
+        ] + [jax.ShapeDtypeStruct(x.shape, full) for x in passed],
         in_specs=[
             pl.BlockSpec((sources, 1, 1, groups, width), lambda e, f: (0, 0, e, 0, 0)),
             pl.BlockSpec((sources, 1, 1, groups, width), lambda e, f: (0, 1, e, 0, 0)),

time: 138 us -> 138 us (level)
  no operation moved by 1% of the time
where the time goes in v3:
time: 138 us
  Pallas kernels  137 us (99%)
    pallas_call x1, Pallas kernels, layer(): pl.pallas_call(functools.partial(layer_body, experts, groups, blocks), ou...  125 us
    pallas_call x1, Pallas kernels, expert_grads(): pl.pallas_call(functools.partial(expert_grad_body, experts, len(passed)),...  11.9 us

profile of v3, /device:TPU:0, one launch (start us, length us, event | category | flops | bytes accessed | tf_op | source)
XLA Modules:
  0.0 137.7 jit_solution(12038091954930653248)
XLA Ops:
  0.6 124.9 %layer.1 = (bf16[128,1536]{1,0:T(8,128)(2,1)}, bf16[128,512]{1,0:T(8,128)(2,1)}, f32[16,128]{1,0:T(8,128)}, f32[512,512]{1,0:T(8,128)}, f32[512,512]{1,0:T(8,128...) custom-call(s32[16]{0:T(128)} %table_ref.1, ...), custom_call_target="tpu_custom_call" | custom-call | flops 149500002304 | bytes 1048576 | tf_op jit(solution)/shard_map/layer/pallas_call | solution.py:1073
  125.6 11.9 %expert_grads.1 = (f32[2,512,2048]{2,1,0:T(8,128)}, f32[2,2048,512]{2,1,0:T(8,128)}, f32[8,128]{1,0:T(8,128)}, f32[1,128]{1,0:T(1,128)}, f32[1,128]{1,0:T(1,128)...) custom-call(bf16[32,2,2,16,512]{4,3,2,1,0:T(8,128)(2,1)} %bitcast.16, ...), custom_call_target="tpu_custom_call" | custom-call | flops 11500000256 | bytes 1048576 | tf_op jit(solution)/shard_map/expert_grads/pallas_call | solution.py:1117
